TPU v7x, 512 devices: a whole 4x8x8 slice. The times are simulated.
512 devices in a mesh: tab: 128 (over z, y, x_hi), col: 4 (over x_lo, core).
Axes of the slice: x: 4 (x_hi: 2, x_lo: 2; x = x_hi * 2 + x_lo), y: 8, z: 8, core: 2. Of those that a mesh axis runs over, the one named last changes fastest.
Arguments:
- pooled: bfloat16 [4096, 128, 512], P('tab', None, 'col'), may hold values from -0.375 to 0.375
- pair_grads: bfloat16 [4096, 8128], P('tab', 'col'), may hold values from -6 to 6
- sample_slot: int32 [4096], replicated, may hold values from 0 to 4095, each once
- table_order: int32 [128], replicated, may hold values from 0 to 127, each once
Outputs:
- table_grads: bfloat16 [128, 4096, 512], P('tab', None, 'col')
Inputs may be any that keep to these rules, and one draw needn't show every extreme that they name: Sample b sits at row sample_slot[b] of the arrays in owner order; every row holds one sample. Index k of tab owns table table_order[k]; each table once.
All inputs are finite; a program needn't handle non-finite values.
Results may differ from a plain program's by a relative error of at most 0.001.
Values may be sent and summed in bfloat16 or wider, within the bound.
A program may use at most 64 MiB of HBM per device.

v0:
```python
import jax
import jax.numpy as jnp
import numpy as np
from jax import lax
from jax.sharding import PartitionSpec as P


def pair_table(count):
    row_ids = np.arange(count)[:, None]
    col_ids = np.arange(count)[None, :]
    larger = np.maximum(row_ids, col_ids)
    smaller = np.minimum(row_ids, col_ids)
    table = larger * (larger - 1) // 2 + smaller
    table = np.where(row_ids == col_ids, count * (count - 1) // 2, table)
    return table.astype(np.int32)


def per_device(pooled, pair_grads, sample_slot, table_order):
    tables = pooled.shape[1]
    pair_count = tables * (tables - 1) // 2
    rows_here = pooled.shape[0]
    pair_width = pair_grads.shape[1]
    table = jnp.asarray(pair_table(tables))[table_order].reshape(-1).astype(jnp.int32)
    shifted = table - lax.axis_index("col") * pair_width
    inside = (table < pair_count) & (shifted >= 0) & (shifted < pair_width)
    column = jnp.where(inside, shifted, pair_width)
    padded = jnp.concatenate([pair_grads, jnp.zeros((rows_here, 1), jnp.bfloat16)], axis=1)
    partial_tiles = jnp.take(padded, column, axis=1).astype(jnp.float32)
    tiles = lax.psum(partial_tiles.astype(jnp.bfloat16), "col")
    tiles = tiles.reshape(rows_here, tables, tables)
    grads = jnp.einsum("bij,bjd->ibd", tiles, pooled, preferred_element_type=jnp.float32).astype(
        jnp.bfloat16
    )
    received = lax.all_to_all(grads, "tab", split_axis=0, concat_axis=1, tiled=True)
    return jnp.take(received, sample_slot, axis=1)


def solution(mesh):
    placed = (P("tab", None, "col"), P("tab", "col"), P(), P())
    return jax.shard_map(
        per_device, mesh=mesh, in_specs=placed, out_specs=P("tab", None, "col"), check_vma=False
    )
```

profile of v0, /device:TPU:8, one launch (start us, length us, event | category | flops | bytes accessed | tf_op | source)
XLA Modules:
  0.0 215.4 jit_solution(428191872638450061)
XLA Ops:
  6.5 0.0 copy-start
  6.5 0.0 all-reduce.3.cloned.1.call-start
  6.5 0.7 compare_select_fusion.3
  7.3 1.5 gather_fusion
  8.8 0.1 compare_and_fusion
  8.8 0.2 compare_select_fusion
  9.1 1.2 copy.11
  10.3 0.1 concatenate.3
  10.4 57.4 %gather_fusion.1 = bf16[16384,32]{1,0:T(8,128)(2,1)} fusion(bf16[32,2033]{0,1:T(8,128)(2,1)S(1)} %concatenate.3, s32[16384]{0:T(1024)S(1)} %broadcast_clamp_fusion), kind=kCustom, calls=%fused_computation.1 | custom fusion | bytes 2162688 | tf_op jit(solution)/shard_map/jit(_take)/gather | solution.py:28
  67.8 11.5 %broadcast_select_fusion = bf16[16384,32]{1,0:T(8,128)(2,1)} fusion(bf16[16384,32]{1,0:T(8,128)(2,1)} %gather_fusion.1, pred[16384]{0:T(1024)(128)(4,1)S(1)} %get-tuple-element.5), kind=kLoop, calls=%fused_computation.3 | loop fusion | flops 524288 | bytes 2113536 | tf_op jit(solution)/shard_map/jit(_take)/select_n | solution.py:28
  79.3 4.8 %copy.14 = bf16[32,128,128]{2,1,0:T(8,128)(2,1)} copy(bf16[32,128,128]{0,2,1:T(8,128)(2,1)} %bitcast.44) | data formatting | bytes 2097152 | tf_op jit(solution)/shard_map/reshape | solution.py:30
  84.1 0.0 copy-start.1
  84.1 0.0 all-reduce.3.cloned.1.call-update
  84.2 56.9 %all-reduce.3.cloned.1.call-done = bf16[32,128,128]{2,1,0:T(8,128)(2,1)} async-done(((bf16[32,128,128]{2,1,0:T(8,128)(2,1)}), bf16[32,128,128]{2,1,0:T(8,128)(2,1)}) %all-reduce.3.cloned.1.call-update) | async-done | bytes 1048592 | tf_op jit(solution)/shard_map/psum | solution.py:29
  141.1 0.0 copy-done
  141.1 1.7 fusion
  142.7 1.6 copy.13
  144.4 16.3 %all-to-all-start = ((bf16[128,32,128]{2,1,0:T(8,128)(2,1)}), bf16[128,32,128]{2,1,0:T(8,128)(2,1)S(1)}, u32[]{:S(2)}, u32[]{:S(2)}) async-start(bf16[128,32,128]{2,1,0:T(8,128)(2,1)} %copy.13), calls=%async_computation | async-start | bytes 2097152 | tf_op jit(solution)/shard_map/all_to_all | solution.py:34
  160.7 0.0 copy-done.1
  160.7 32.8 %all-to-all-done = bf16[128,32,128]{2,1,0:T(8,128)(2,1)S(1)} async-done(((bf16[128,32,128]{2,1,0:T(8,128)(2,1)}), bf16[128,32,128]{2,1,0:T(8,128)(2,1)S(1)}, u32[]{:S(2)}, u32[]{:S(2)}) %all-to-all-start) | async-done | bytes 1048608 | tf_op jit(solution)/shard_map/all_to_all | solution.py:34
  193.5 12.1 %gather_fusion.2 = bf16[4096,128]{1,0:T(8,128)(2,1)S(1)} fusion(bf16[4096,128]{1,0:T(8,128)(2,1)S(1)} %bitcast.43, s32[4096]{0:T(1024)S(1)} %fusion.5), kind=kCustom, calls=%fused_computation.2 | custom fusion | bytes 2113536 | tf_op jit(solution)/shard_map/jit(_take)/gather | solution.py:35
  205.7 2.9 %bitcast_select_fusion = bf16[1,4096,128]{2,1,0:T(8,128)(2,1)} fusion(bf16[4096,128]{1,0:T(8,128)(2,1)S(1)} %gather_fusion.2, pred[4096]{0:T(1024)(128)(4,1)S(1)} %compare_and_fusion.1), kind=kLoop, calls=%fused_computation.6 | loop fusion | flops 524288 | bytes 2101248 | tf_op jit(solution)/shard_map/jit(_take)/select_n | solution.py:35
  (4 shorter events, 0.0 us)
Async XLA Ops:
  6.5 134.5 %copy-start = (bf16[32,128,128]{2,1,0:T(8,128)(2,1)S(1)}, bf16[32,128,128]{2,1,0:T(8,128)(2,1)}, u32[]{:S(2)}) copy-start(bf16[32,128,128]{2,1,0:T(8,128)(2,1)} %param.5) | copy-start | bytes 3145732
  6.5 134.5 %all-reduce.3.cloned.1.call-start = ((), (), s32[]{:S(2)}) async-start(), calls=%async_computation.1 | async-start | bytes 2097152 | tf_op jit(solution)/shard_map/psum | solution.py:29
  84.1 76.5 %copy-start.1 = (s32[4096]{0:T(1024)S(1)}, s32[4096]{0:T(1024)}, u32[]{:S(2)}) copy-start(s32[4096]{0:T(1024)} %param.7) | copy-start | bytes 49156
  144.4 49.2 %all-to-all-start = ((bf16[128,32,128]{2,1,0:T(8,128)(2,1)}), bf16[128,32,128]{2,1,0:T(8,128)(2,1)S(1)}, u32[]{:S(2)}, u32[]{:S(2)}) async-start(bf16[128,32,128]{2,1,0:T(8,128)(2,1)} %copy.13), calls=%async_computation | async-start | bytes 2097152 | tf_op jit(solution)/shard_map/all_to_all | solution.py:34
Sparse Core Ops, SparseCore 0:
  84.3 56.7 all-reduce.2
where the time goes:
time: 216 us; the launch traced here: 215 us
  waiting for transfers between devices  89.8 us (42%)
  local copies, waits for them, and re-layouts  78.8 us (36%)
  starting transfers between devices  16.3 us (8%)
  other arithmetic  15.4 us (7%)
  between operations  13.5 us (6%)
    gather x1, local copies, waits for them, and re-layouts, per_device(): partial_tiles = jnp.take(padded, column, axis=1).astype(jnp.float32)  57.4 us
    psum x1, waiting for transfers between devices, per_device(): tiles = lax.psum(partial_tiles.astype(jnp.bfloat16), 'col')  56.9 us
    all_to_all x1, waiting for transfers between devices, per_device(): lax.all_to_all(grads, 'tab', split_axis=0, concat_axis=1, tiled=True)  32.8 us
    all_to_all x1, starting transfers between devices, per_device(): lax.all_to_all(grads, 'tab', split_axis=0, concat_axis=1, tiled=True)  16.3 us
    gather x1, local copies, waits for them, and re-layouts, per_device(): return jnp.take(received, sample_slot, axis=1)  12.1 us
    select_n x2, other arithmetic, per_device(): partial_tiles = jnp.take(padded, column, axis=1).astype(jnp.float32)  11.7 us
    reshape x1, local copies, waits for them, and re-layouts, per_device(): tiles = tiles.reshape(rows_here, tables, tables)  4.83 us
  transfers between devices with their start and end apart: 2, of which 2 were waited for; matrix products, arithmetic and copies ran while one was open for 0% of the time, Pallas kernels for 0%

commit v1 on v0

v1 whole, which is shorter than its diff:
```python
import functools

import jax
import jax.numpy as jnp
from jax import lax
from jax.experimental import pallas as pl
from jax.experimental.pallas import tpu as pltpu
from jax.sharding import PartitionSpec as P

MESH = pl.DeviceIdType.MESH
LANES = 128
SIGNALS_A_STEP = 8


def row_pieces(a, quarter):
    at, here, left, out = a * (a - 1) // 2, 0, a, []
    while left:
        part, local = at // quarter, at % quarter
        tile, lane = local // LANES, local % LANES
        count = min(left, quarter - local, LANES - lane)
        out.append((part, tile, lane, here, count))
        at, here, left = at + count, here + count, left - count
    return out


def exchange(tabs, cols, pooled, pairs_in, order, out, pairs, lower, grads, send, pair_send, pair_recv, row_send, row_recv):
    rows, tables, _ = pooled.shape
    quarter = pairs_in.shape[1]
    me, col = lax.axis_index("tab"), lax.axis_index("col")

    barrier = pltpu.get_barrier_semaphore()
    for k in range(1, cols):
        pl.semaphore_signal(barrier, inc=1, device_id={"col": (col + k) % cols}, device_id_type=MESH)

    def greet(i, carry):
        pl.semaphore_signal(barrier, inc=1, device_id={"tab": (me + i) % tabs}, device_id_type=MESH)
        return carry

    lax.fori_loop(1, tabs, greet, 0)
    pl.semaphore_wait(barrier, tabs + cols - 2)

    copies = []
    for k in range(1, cols):
        copy = pltpu.make_async_remote_copy(
            src_ref=pairs_in,
            dst_ref=pairs.at[col],
            send_sem=pair_send.at[k - 1],
            recv_sem=pair_recv.at[k - 1],
            device_id={"col": (col + k) % cols},
            device_id_type=MESH,
        )
        copy.start()
        copies.append(copy)
    pairs[col] = pairs_in[...]
    for copy in copies:
        copy.wait()

    lane = lax.broadcasted_iota(jnp.int32, (rows, LANES), 1)
    lower[pl.ds(0, rows, stride=tables), :] = jnp.zeros((rows, LANES), jnp.float32)
    for a in range(1, tables):
        row = jnp.zeros((rows, LANES), jnp.float32)
        for part, tile, there, here, count in row_pieces(a, quarter):
            width = min(LANES, quarter - tile * LANES)
            piece = pairs[part, :, tile * LANES : tile * LANES + width].astype(jnp.float32)
            if width < LANES:
                piece = jnp.concatenate([piece, jnp.zeros((rows, LANES - width), jnp.float32)], axis=1)
            shift = (here - there) % LANES
            if shift:
                piece = pltpu.roll(piece, shift, 1)
            row = jnp.where((lane >= here) & (lane < here + count), piece, row)
        lower[pl.ds(a, rows, stride=tables), :] = row

    flat = grads.reshape(tables * rows, LANES)

    def multiply(r, carry):
        half = lower[pl.ds(pl.multiple_of(r * tables, tables), tables), :]
        both = (half + half.T).astype(jnp.bfloat16)
        flat[pl.ds(r, tables, stride=rows), :] = jnp.dot(both, pooled[r], preferred_element_type=jnp.float32)
        return carry

    lax.fori_loop(0, rows, multiply, 0)

    def place(k, carry):
        send[k] = grads[order[k]].astype(jnp.bfloat16)
        return carry

    lax.fori_loop(0, tables, place, 0)

    def start(i, carry):
        to = (me + i * 45) % tabs
        pltpu.make_async_remote_copy(
            src_ref=send.at[to],
            dst_ref=out.at[me],
            send_sem=row_send,
            recv_sem=row_recv,
            device_id={"tab": to},
            device_id_type=MESH,
        ).start()
        return carry

    lax.fori_loop(1, tabs, start, 0)
    out[me] = send[me]
    others = out.at[pl.ds(0, tabs - 1)]
    pltpu.make_async_copy(others, others, row_recv).wait()
    sent = send.at[pl.ds(0, tabs - 1)]
    pltpu.make_async_copy(sent, sent, row_send).wait()


def reorder(slot, rows_in, out, wide, picked):
    wide[...] = rows_in[...].astype(jnp.float32)

    def step(i, carry):
        for u in range(16):
            b = i * 16 + u
            picked[pl.ds(b, 1), :] = wide[pl.ds(slot[b], 1), :]
        return carry

    lax.fori_loop(0, out.shape[0] // 16, step, 0)
    out[...] = picked[...].astype(out.dtype)


def per_device(tabs, cols, pooled, pair_grads, sample_slot, table_order):
    rows, tables, width = pooled.shape
    vmem = pl.BlockSpec(memory_space=pltpu.VMEM)
    smem = pl.BlockSpec(memory_space=pltpu.SMEM)
    received = pl.pallas_call(
        functools.partial(exchange, tabs, cols),
        out_shape=jax.ShapeDtypeStruct((tabs, rows, width), jnp.bfloat16),
        in_specs=[vmem, vmem, smem],
        out_specs=vmem,
        scratch_shapes=[
            pltpu.VMEM((cols,) + pair_grads.shape, jnp.bfloat16),
            pltpu.VMEM((rows * tables, LANES), jnp.float32),
            pltpu.VMEM((tables, rows, width), jnp.float32),
            pltpu.VMEM((tables, rows, width), jnp.bfloat16),
            pltpu.SemaphoreType.DMA((cols - 1,)),
            pltpu.SemaphoreType.DMA((cols - 1,)),
            pltpu.SemaphoreType.DMA,
            pltpu.SemaphoreType.DMA,
        ],
        compiler_params=pltpu.CompilerParams(collective_id=0, has_side_effects=True, vmem_limit_bytes=32 << 20),
        name="exchange",
    )(pooled, pair_grads, table_order)
    total = tabs * rows
    ordered = pl.pallas_call(
        reorder,
        out_shape=jax.ShapeDtypeStruct((total, width), jnp.bfloat16),
        in_specs=[smem, vmem],
        out_specs=vmem,
        scratch_shapes=[pltpu.VMEM((total, width), jnp.float32), pltpu.VMEM((total, width), jnp.float32)],
        compiler_params=pltpu.CompilerParams(vmem_limit_bytes=32 << 20),
        name="reorder",
    )(sample_slot, received.reshape(total, width))
    return ordered.reshape(1, total, width)


def solution(mesh):
    placed = (P("tab", None, "col"), P("tab", "col"), P(), P())
    return jax.shard_map(
        functools.partial(per_device, mesh.shape["tab"], mesh.shape["col"]),
        mesh=mesh,
        in_specs=placed,
        out_specs=P("tab", None, "col"),
        check_vma=False,
    )
```

time: 216 us -> 73.5 us (0.34)
  the two profiles are of different devices: /device:TPU:8 before, /device:TPU:1 now
where the time goes in v1:
time: 73.5 us; the launch traced here: 73.3 us
  Pallas kernels  70.5 us (96%)
  local copies, waits for them, and re-layouts  2.79 us (4%)
    pallas_call x1, Pallas kernels, per_device(): pl.pallas_call(functools.partial(exchange, tabs, cols), out_shape=jax.Sha...  64 us
    pallas_call x1, Pallas kernels, per_device(): pl.pallas_call(reorder, out_shape=jax.ShapeDtypeStruct((total, width), jn...  6.46 us
    unnamed x8, local copies, waits for them, and re-layouts  2.79 us

profile of v1, /device:TPU:1, one launch (start us, length us, event | category | flops | bytes accessed | tf_op | source)
XLA Modules:
  0.0 73.3 jit_solution(17650324863846656526)
XLA Ops:
  0.0 0.0 copy-start
  0.0 1.2 %copy-done = bf16[32,128,128]{2,1,0:T(8,128)(2,1)S(1)} copy-done((bf16[32,128,128]{2,1,0:T(8,128)(2,1)S(1)}, bf16[32,128,128]{2,1,0:T(8,128)(2,1)}, u32[]{:S(2)}) %copy-start) | copy-done | bytes 1048600
  1.2 0.0 copy-start.1
  1.2 0.9 %copy-done.1 = bf16[32,2032]{1,0:T(8,128)(2,1)S(1)} copy-done((bf16[32,2032]{1,0:T(8,128)(2,1)S(1)}, bf16[32,2032]{1,0:T(8,128)(2,1)}, u32[]{:S(2)}) %copy-start.1) | copy-done | bytes 130072
  2.1 0.0 copy-start.3
  2.1 0.7 copy-done.3
  2.8 0.0 copy-start.2
  2.8 64.0 %exchange.1 = bf16[128,32,128]{2,1,0:T(8,128)(2,1)S(1)} custom-call(bf16[32,128,128]{2,1,0:T(8,128)(2,1)S(1)} %copy-done, bf16[32,2032]{1,0:T(8,128)(2,1)S(1)} %copy-done.1, s32[128]{0:T(128)S(1)} %copy-done.3), custom_call_target="tpu_custom_call" | custom-call | tf_op jit(solution)/shard_map/exchange/pallas_call | solution.py:126
  66.8 0.0 copy-done.2
  66.8 6.5 %reorder.1 = bf16[4096,128]{1,0:T(8,128)(2,1)} custom-call(s32[4096]{0:T(1024)S(1)} %copy-done.2, bf16[4096,128]{1,0:T(8,128)(2,1)S(1)} %bitcast.2), custom_call_target="tpu_custom_call" | custom-call | tf_op jit(solution)/shard_map/reorder/pallas_call | solution.py:145
Async XLA Ops:
  0.0 1.2 %copy-start = (bf16[32,128,128]{2,1,0:T(8,128)(2,1)S(1)}, bf16[32,128,128]{2,1,0:T(8,128)(2,1)}, u32[]{:S(2)}) copy-start(bf16[32,128,128]{2,1,0:T(8,128)(2,1)} %pooled.1) | copy-start | bytes 3145732
  1.2 0.9 %copy-start.1 = (bf16[32,2032]{1,0:T(8,128)(2,1)S(1)}, bf16[32,2032]{1,0:T(8,128)(2,1)}, u32[]{:S(2)}) copy-start(bf16[32,2032]{1,0:T(8,128)(2,1)} %pairs_in.1) | copy-start | bytes 390148
  2.1 0.7 copy-start.3
  2.8 64.0 %copy-start.2 = (s32[4096]{0:T(1024)S(1)}, s32[4096]{0:T(1024)}, u32[]{:S(2)}) copy-start(s32[4096]{0:T(1024)} %slot.1) | copy-start | bytes 49156

commit v2 on v0

v2 whole, which is shorter than its diff:
```python
import functools

import jax
import jax.numpy as jnp
from jax import lax
from jax.experimental import pallas as pl
from jax.experimental.pallas import tpu as pltpu
from jax.sharding import PartitionSpec as P

MESH = pl.DeviceIdType.MESH
LANES = 128
PART = 16
SENDERS = 32
BLOCK = 1024
STRIDE = 77


def row_pieces(a, quarter):
    at, here, left, out = a * (a - 1) // 2, 0, a, []
    while left:
        part, local = at // quarter, at % quarter
        tile, lane = local // LANES, local % LANES
        count = min(left, quarter - local, LANES - lane)
        out.append((part, tile, lane, here, count))
        at, here, left = at + count, here + count, left - count
    return out


def by_distance():
    offsets = [(dz, dy, dx) for dz in range(8) for dy in range(8) for dx in range(2)][1:]
    return sorted(offsets, key=lambda o: -(min(o[0], 8 - o[0]) + min(o[1], 8 - o[1]) + 2 * o[2]))


def exchange(
    tabs, pooled_in, pairs_in, slot_in, order_in, out, pairs, pooled, slot, order, lower, grads, send, landed, wide, total,
    own_sem, pooled_sem, slot_sem, order_sem, pair_send, pair_recv, row_send, row_recv,
):
    rows, tables, _ = pooled.shape
    quarter = pairs.shape[2]
    parts = rows // PART
    me, col = lax.axis_index("tab"), lax.axis_index("col")
    sibling = col + 1 - 2 * (col % 2)
    across = (col + 2) % 4

    own = pltpu.make_async_copy(pairs_in, pairs.at[col], own_sem)
    get_pooled = pltpu.make_async_copy(pooled_in, pooled, pooled_sem)
    get_slot = pltpu.make_async_copy(slot_in, slot, slot_sem)
    get_order = pltpu.make_async_copy(order_in, order, order_sem)
    own.start()
    get_pooled.start()
    get_order.start()
    get_slot.start()

    barrier = pltpu.get_barrier_semaphore()
    for peer in (across, sibling):
        pl.semaphore_signal(barrier, inc=1, device_id={"col": peer}, device_id_type=MESH)
    z, y, x = me // 16, (me // 2) % 8, me % 2
    for dz, dy, dx in by_distance():
        to = ((z + dz) % 8) * 16 + ((y + dy) % 8) * 2 + (x + dx) % 2
        pl.semaphore_signal(barrier, inc=1, device_id={"tab": to}, device_id_type=MESH)
    own.wait()
    pl.semaphore_wait(barrier, tabs + 1)

    def pass_pairs(lane, part, slot, peer):
        copy = pltpu.make_async_remote_copy(
            src_ref=pairs.at[slot, pl.ds(part * PART, PART)],
            dst_ref=pairs.at[slot, pl.ds(part * PART, PART)],
            send_sem=pair_send.at[lane, part],
            recv_sem=pair_recv.at[lane, part],
            device_id={"col": peer},
            device_id_type=MESH,
        )
        copy.start()
        return copy

    direct = [pass_pairs(0, p, col, across) for p in range(parts)]
    beside = [pass_pairs(1, p, col, sibling) for p in range(parts)]
    passed = []
    direct[0].wait_recv()
    passed.append(pass_pairs(2, 0, across, sibling))

    lane = lax.broadcasted_iota(jnp.int32, (PART, LANES), 1)
    flat = grads.reshape(tables * rows, LANES)
    groups = tabs // SENDERS

    def rows_of(part, i):
        return landed.at[part * groups + i // SENDERS, pl.ds(pl.multiple_of((i % SENDERS) * PART, PART), PART)]

    def multiply(r, carry):
        half = lower[pl.ds(pl.multiple_of(r * tables, tables), tables), :]
        both = (half + half.T).astype(jnp.bfloat16)
        flat[pl.ds(r, tables, stride=rows), :] = jnp.dot(both, pooled[r], preferred_element_type=jnp.float32)
        return carry

    for part in range(parts):
        span = pl.ds(part * PART, PART)
        beside[part].wait_recv()
        passed[part].wait_recv()
        lower[pl.ds(part * PART * tables, PART, stride=tables), :] = jnp.zeros((PART, LANES), jnp.float32)
        for a in range(1, tables):
            row = jnp.zeros((PART, LANES), jnp.float32)
            for source, tile, there, first, count in row_pieces(a, quarter):
                width = min(LANES, quarter - tile * LANES)
                piece = pairs[source, span, tile * LANES : tile * LANES + width].astype(jnp.float32)
                if width < LANES:
                    piece = jnp.concatenate([piece, jnp.zeros((PART, LANES - width), jnp.float32)], axis=1)
                shift = (first - there) % LANES
                if shift:
                    piece = pltpu.roll(piece, shift, 1)
                row = jnp.where((lane >= first) & (lane < first + count), piece, row)
            lower[pl.ds(part * PART * tables + a, PART, stride=tables), :] = row
        if part + 1 < parts:
            direct[part + 1].wait_recv()
            passed.append(pass_pairs(2, part + 1, across, sibling))
        if part == 0:
            get_pooled.wait()
            get_order.wait()
        lax.fori_loop(part * PART, (part + 1) * PART, multiply, 0, unroll=8)

        def place(k, carry):
            send[k, span] = grads[order[k]][part * PART : (part + 1) * PART].astype(jnp.bfloat16)
            return carry

        lax.fori_loop(0, tables, place, 0, unroll=8)

        def start(i, carry):
            to = (me + i * STRIDE) % tabs
            pltpu.make_async_remote_copy(
                src_ref=send.at[to, span],
                dst_ref=rows_of(part, i),
                send_sem=row_send.at[part],
                recv_sem=row_recv.at[part * groups + i // SENDERS],
                device_id={"tab": to},
                device_id_type=MESH,
            ).start()
            return carry

        lax.fori_loop(1, tabs, start, 0)
        pltpu.make_async_copy(send.at[me, span], rows_of(part, 0), row_recv.at[part * groups]).start()

    get_slot.wait()
    for i in range(slot.shape[0]):
        wide[pl.ds(i * LANES, LANES), :] = jnp.broadcast_to(slot[pl.ds(i, 1), :], (LANES, LANES)).T
    total[...] = jnp.zeros_like(total)

    lane_id = lax.broadcasted_iota(jnp.int32, (1, LANES), 1)

    def add_group(g, carry):
        pltpu.make_async_copy(landed.at[g], landed.at[g], row_recv.at[g]).wait()
        first = (g % groups) * SENDERS
        held = landed[g]
        row_ids = []
        for t in range(SENDERS * PART // LANES):
            step = first + t * (LANES // PART) + lane_id // PART
            sender = (me - step * STRIDE + tabs * STRIDE) % tabs
            row_ids.append(sender * rows + (g // groups) * PART + lane_id % PART)

        def add(b, c):
            at = pl.ds(pl.multiple_of(b * BLOCK, BLOCK), BLOCK)
            wanted = wide[at, :]
            picks = jnp.concatenate(
                [jnp.where(wanted == ids, jnp.bfloat16(1), jnp.bfloat16(0)) for ids in row_ids], axis=1
            )
            total[at, :] += jnp.dot(picks, held, preferred_element_type=jnp.float32)
            return c

        lax.fori_loop(0, tabs * rows // BLOCK, add, 0, unroll=4)
        return carry

    lax.fori_loop(0, parts * groups, add_group, 0)
    out[...] = total[...].astype(out.dtype)

    for part in range(parts):
        direct[part].wait_send()
        beside[part].wait_send()
        passed[part].wait_send()
        sent = send.at[pl.ds(0, tabs - 1), pl.ds(part * PART, PART)]
        pltpu.make_async_copy(sent, sent, row_send.at[part]).wait()


def per_device(tabs, cols, pooled, pair_grads, sample_slot, table_order):
    rows, tables, width = pooled.shape
    vmem = pl.BlockSpec(memory_space=pltpu.VMEM)
    here = pl.BlockSpec(memory_space=pltpu.HBM)
    parts = rows // PART
    total = tabs * rows
    groups = parts * tabs // SENDERS
    ordered = pl.pallas_call(
        functools.partial(exchange, tabs),
        out_shape=jax.ShapeDtypeStruct((total, width), jnp.bfloat16),
        in_specs=[here] * 4,
        out_specs=vmem,
        scratch_shapes=[
            pltpu.VMEM((cols,) + pair_grads.shape, jnp.bfloat16),
            pltpu.VMEM(pooled.shape, jnp.bfloat16),
            pltpu.VMEM((total // LANES, LANES), jnp.int32),
            pltpu.SMEM((tables,), jnp.int32),
            pltpu.VMEM((rows * tables, LANES), jnp.float32),
            pltpu.VMEM((tables, rows, width), jnp.float32),
            pltpu.VMEM((tables, rows, width), jnp.bfloat16),
            pltpu.VMEM((groups, SENDERS * PART, width), jnp.bfloat16),
            pltpu.VMEM((total, LANES), jnp.int32),
            pltpu.VMEM((total, width), jnp.float32),
            pltpu.SemaphoreType.DMA,
            pltpu.SemaphoreType.DMA,
            pltpu.SemaphoreType.DMA,
            pltpu.SemaphoreType.DMA,
            pltpu.SemaphoreType.DMA((3, parts)),
            pltpu.SemaphoreType.DMA((3, parts)),
            pltpu.SemaphoreType.DMA((parts,)),
            pltpu.SemaphoreType.DMA((groups,)),
        ],
        compiler_params=pltpu.CompilerParams(collective_id=0, has_side_effects=True, vmem_limit_bytes=60 << 20),
        name="exchange",
    )(pooled, pair_grads, sample_slot.reshape(total // LANES, LANES), table_order)
    return ordered.reshape(1, total, width)


def solution(mesh):
    placed = (P("tab", None, "col"), P("tab", "col"), P(), P())
    return jax.shard_map(
        functools.partial(per_device, mesh.shape["tab"], mesh.shape["col"]),
        mesh=mesh,
        in_specs=placed,
        out_specs=P("tab", None, "col"),
        check_vma=False,
    )
```

time: 216 us -> 57.8 us (0.27)
  the two profiles are of different devices: /device:TPU:8 before, /device:TPU:1 now
where the time goes in v2:
time: 57.8 us; the launch traced here: 57.6 us
  Pallas kernels  55.4 us (96%)
  local copies, waits for them, and re-layouts  2.26 us (4%)
    pallas_call x1, Pallas kernels, per_device(): pl.pallas_call(functools.partial(exchange, tabs), out_shape=jax.ShapeDtyp...  55.4 us
    unnamed x1, local copies, waits for them, and re-layouts  2.26 us

profile of v2, /device:TPU:1, one launch (start us, length us, event | category | flops | bytes accessed | tf_op | source)
XLA Modules:
  0.0 57.6 jit_solution(1708893778944460149)
XLA Ops:
  0.0 55.4 %exchange.1 = bf16[4096,128]{1,0:T(8,128)(2,1)} custom-call(bf16[32,128,128]{2,1,0:T(8,128)(2,1)} %pooled_in.1, bf16[32,2032]{1,0:T(8,128)(2,1)} %pairs_in.1, s32[32,128]{1,0:T(8,128)} %bitcast.3, s32[128]{0:T(128)} %order_in.1), custom_call_target="tpu_custom_call" | custom-call | tf_op jit(solution)/shard_map/exchange/pallas_call | solution.py:188
  55.4 2.3 %copy.6 = bf16[1,4096,128]{2,1,0:T(8,128)(2,1)} copy(bf16[1,4096,128]{2,1,0:T(8,128)(2,1)} %bitcast.2) | data formatting | bytes 2097152

commit v3 on v2

--- a/solution.py
+++ b/solution.py
@@ -10,8 +10,9 @@
 MESH = pl.DeviceIdType.MESH
 LANES = 128
 PART = 16
-SENDERS = 32
+PLANE = 16
 BLOCK = 1024
+SECOND = 4096
 STRIDE = 77
 
 
@@ -26,19 +27,15 @@
     return out
 
 
-def by_distance():
-    offsets = [(dz, dy, dx) for dz in range(8) for dy in range(8) for dx in range(2)][1:]
-    return sorted(offsets, key=lambda o: -(min(o[0], 8 - o[0]) + min(o[1], 8 - o[1]) + 2 * o[2]))
-
-
 def exchange(
     tabs, pooled_in, pairs_in, slot_in, order_in, out, pairs, pooled, slot, order, lower, grads, send, landed, wide, total,
-    own_sem, pooled_sem, slot_sem, order_sem, pair_send, pair_recv, row_send, row_recv,
+    own_sem, pooled_sem, slot_sem, order_sem, pair_send, pair_recv, row_send, row_recv, answers,
 ):
     rows, tables, _ = pooled.shape
     quarter = pairs.shape[2]
     parts = rows // PART
     me, col = lax.axis_index("tab"), lax.axis_index("col")
+    plane = me // PLANE
     sibling = col + 1 - 2 * (col % 2)
     across = (col + 2) % 4
 
@@ -54,12 +51,29 @@
     barrier = pltpu.get_barrier_semaphore()
     for peer in (across, sibling):
         pl.semaphore_signal(barrier, inc=1, device_id={"col": peer}, device_id_type=MESH)
-    z, y, x = me // 16, (me // 2) % 8, me % 2
-    for dz, dy, dx in by_distance():
-        to = ((z + dz) % 8) * 16 + ((y + dy) % 8) * 2 + (x + dx) % 2
-        pl.semaphore_signal(barrier, inc=1, device_id={"tab": to}, device_id_type=MESH)
+
+    def signal_tab(sem, to):
+        pl.semaphore_signal(sem, inc=1, device_id={"tab": to}, device_id_type=MESH)
+
+    def signal_span(sem, first, last):
+        low, high = (first + PLANE - 1) // PLANE, last // PLANE
+
+        def one(to, carry):
+            signal_tab(sem, to)
+            return carry
+
+        def block(p, carry):
+            for k in range(PLANE):
+                signal_tab(sem, p * PLANE + k)
+            return carry
+
+        lax.fori_loop(first, jnp.minimum(low * PLANE, last), one, 0)
+        lax.fori_loop(low, high, block, 0)
+        lax.fori_loop(jnp.maximum(high * PLANE, first), last, one, 0)
+
+    signal_span(barrier, me + 1, tabs)
     own.wait()
-    pl.semaphore_wait(barrier, tabs + 1)
+    pl.semaphore_wait(barrier, me + 2)
 
     def pass_pairs(lane, part, slot, peer):
         copy = pltpu.make_async_remote_copy(
@@ -75,16 +89,15 @@
 
     direct = [pass_pairs(0, p, col, across) for p in range(parts)]
     beside = [pass_pairs(1, p, col, sibling) for p in range(parts)]
+
+    signal_span(answers, 0, me)
     passed = []
     direct[0].wait_recv()
     passed.append(pass_pairs(2, 0, across, sibling))
 
     lane = lax.broadcasted_iota(jnp.int32, (PART, LANES), 1)
     flat = grads.reshape(tables * rows, LANES)
-    groups = tabs // SENDERS
-
-    def rows_of(part, i):
-        return landed.at[part * groups + i // SENDERS, pl.ds(pl.multiple_of((i % SENDERS) * PART, PART), PART)]
+    planes = tabs // PLANE
 
     def multiply(r, carry):
         half = lower[pl.ds(pl.multiple_of(r * tables, tables), tables), :]
@@ -109,36 +122,47 @@
                     piece = pltpu.roll(piece, shift, 1)
                 row = jnp.where((lane >= first) & (lane < first + count), piece, row)
             lower[pl.ds(part * PART * tables + a, PART, stride=tables), :] = row
+        if part == 0:
+            get_pooled.wait()
+            get_order.wait()
+        lax.fori_loop(part * PART, (part + 1) * PART, multiply, 0, unroll=8)
+
+        def place(k, carry):
+            send[k, span] = grads[order[k]][part * PART : (part + 1) * PART].astype(jnp.bfloat16)
+            return carry
+
+        lax.fori_loop(0, tables, place, 0, unroll=8)
+
         if part + 1 < parts:
             direct[part + 1].wait_recv()
             passed.append(pass_pairs(2, part + 1, across, sibling))
         if part == 0:
-            get_pooled.wait()
-            get_order.wait()
-        lax.fori_loop(part * PART, (part + 1) * PART, multiply, 0, unroll=8)
-
-        def place(k, carry):
-            send[k, span] = grads[order[k]][part * PART : (part + 1) * PART].astype(jnp.bfloat16)
-            return carry
-
-        lax.fori_loop(0, tables, place, 0, unroll=8)
+
+            @pl.when(me < tabs - 1)
+            def _():
+                pl.semaphore_wait(answers, tabs - 1 - me)
+
 
         def start(i, carry):
             to = (me + i * STRIDE) % tabs
             pltpu.make_async_remote_copy(
                 src_ref=send.at[to, span],
-                dst_ref=rows_of(part, i),
+                dst_ref=landed.at[part, me],
                 send_sem=row_send.at[part],
-                recv_sem=row_recv.at[part * groups + i // SENDERS],
+                recv_sem=row_recv.at[part * planes + plane],
                 device_id={"tab": to},
                 device_id_type=MESH,
             ).start()
             return carry
 
         lax.fori_loop(1, tabs, start, 0)
-        pltpu.make_async_copy(send.at[me, span], rows_of(part, 0), row_recv.at[part * groups]).start()
+        pltpu.make_async_copy(send.at[me, span], landed.at[part, me], row_recv.at[part * planes + plane]).start()
 
     get_slot.wait()
+    at = slot[...]
+    key = (at // PART % parts) * (tabs * PART // 2) + at // (2 * PLANE * rows) * (PLANE * PART)
+    key += at // rows % PLANE * PART + at % PART
+    slot[...] = key + at // (PLANE * rows) % 2 * SECOND
     for i in range(slot.shape[0]):
         wide[pl.ds(i * LANES, LANES), :] = jnp.broadcast_to(slot[pl.ds(i, 1), :], (LANES, LANES)).T
     total[...] = jnp.zeros_like(total)
@@ -146,28 +170,32 @@
     lane_id = lax.broadcasted_iota(jnp.int32, (1, LANES), 1)
 
     def add_group(g, carry):
-        pltpu.make_async_copy(landed.at[g], landed.at[g], row_recv.at[g]).wait()
-        first = (g % groups) * SENDERS
-        held = landed[g]
-        row_ids = []
-        for t in range(SENDERS * PART // LANES):
-            step = first + t * (LANES // PART) + lane_id // PART
-            sender = (me - step * STRIDE + tabs * STRIDE) % tabs
-            row_ids.append(sender * rows + (g // groups) * PART + lane_id % PART)
+        part, p = g // (planes // 2), g % (planes // 2) * 2
+        held = []
+        for q in range(2):
+            at = pl.ds((p + q) * PLANE, PLANE)
+            group = landed.at[part, at]
+            pltpu.make_async_copy(group, group, row_recv.at[part * planes + p + q]).wait()
+            held.append(landed[part, at].reshape(PLANE * PART, LANES))
+        held = jnp.concatenate(held, axis=1)
+        row_ids = [lane_id + (g * PLANE * PART + t * LANES) for t in range(PLANE * PART // LANES)]
 
         def add(b, c):
             at = pl.ds(pl.multiple_of(b * BLOCK, BLOCK), BLOCK)
             wanted = wide[at, :]
+            second = wanted >= SECOND
+            wanted = jnp.where(second, wanted - SECOND, wanted)
             picks = jnp.concatenate(
                 [jnp.where(wanted == ids, jnp.bfloat16(1), jnp.bfloat16(0)) for ids in row_ids], axis=1
             )
-            total[at, :] += jnp.dot(picks, held, preferred_element_type=jnp.float32)
+            both = jnp.dot(picks, held, preferred_element_type=jnp.float32)
+            total[at, :] += jnp.where(second, both[:, LANES:], both[:, :LANES])
             return c
 
         lax.fori_loop(0, tabs * rows // BLOCK, add, 0, unroll=4)
         return carry
 
-    lax.fori_loop(0, parts * groups, add_group, 0)
+    lax.fori_loop(0, parts * planes // 2, add_group, 0)
     out[...] = total[...].astype(out.dtype)
 
     for part in range(parts):
@@ -184,7 +212,6 @@
     here = pl.BlockSpec(memory_space=pltpu.HBM)
     parts = rows // PART
     total = tabs * rows
-    groups = parts * tabs // SENDERS
     ordered = pl.pallas_call(
         functools.partial(exchange, tabs),
         out_shape=jax.ShapeDtypeStruct((total, width), jnp.bfloat16),
@@ -198,7 +225,7 @@
             pltpu.VMEM((rows * tables, LANES), jnp.float32),
             pltpu.VMEM((tables, rows, width), jnp.float32),
             pltpu.VMEM((tables, rows, width), jnp.bfloat16),
-            pltpu.VMEM((groups, SENDERS * PART, width), jnp.bfloat16),
+            pltpu.VMEM((parts, tabs, PART, width), jnp.bfloat16),
             pltpu.VMEM((total, LANES), jnp.int32),
             pltpu.VMEM((total, width), jnp.float32),
             pltpu.SemaphoreType.DMA,
@@ -208,7 +235,8 @@
             pltpu.SemaphoreType.DMA((3, parts)),
             pltpu.SemaphoreType.DMA((3, parts)),
             pltpu.SemaphoreType.DMA((parts,)),
-            pltpu.SemaphoreType.DMA((groups,)),
+            pltpu.SemaphoreType.DMA((parts * tabs // PLANE,)),
+            pltpu.SemaphoreType.REGULAR,
         ],
         compiler_params=pltpu.CompilerParams(collective_id=0, has_side_effects=True, vmem_limit_bytes=60 << 20),
         name="exchange",

time: 57.8 us -> 56 us (0.969)
  the two profiles are of different devices: /device:TPU:1 before, /device:TPU:8 now
where the time goes in v3:
time: 56 us; the launch traced here: 55.8 us
  Pallas kernels  53.6 us (96%)
  local copies, waits for them, and re-layouts  2.26 us (4%)
    pallas_call x1, Pallas kernels, per_device(): pl.pallas_call(functools.partial(exchange, tabs), out_shape=jax.ShapeDtyp...  53.6 us
    unnamed x1, local copies, waits for them, and re-layouts  2.26 us

profile of v3, /device:TPU:8, one launch (start us, length us, event | category | flops | bytes accessed | tf_op | source)
XLA Modules:
  0.0 55.8 jit_solution(7161864795028076057)
XLA Ops:
  0.0 53.6 %exchange.1 = bf16[4096,128]{1,0:T(8,128)(2,1)} custom-call(bf16[32,128,128]{2,1,0:T(8,128)(2,1)} %pooled_in.1, bf16[32,2032]{1,0:T(8,128)(2,1)} %pairs_in.1, s32[32,128]{1,0:T(8,128)} %bitcast.3, s32[128]{0:T(128)} %order_in.1), custom_call_target="tpu_custom_call" | custom-call | tf_op jit(solution)/shard_map/exchange/pallas_call | solution.py:215
  53.6 2.3 %copy.6 = bf16[1,4096,128]{2,1,0:T(8,128)(2,1)} copy(bf16[1,4096,128]{2,1,0:T(8,128)(2,1)} %bitcast.2) | data formatting | bytes 2097152

commit v4 on v3

--- a/solution.py
+++ b/solution.py
@@ -27,6 +27,16 @@
     return out
 
 
+def by_distance():
+    groups = {}
+    for dz in range(8):
+        for dy in range(8):
+            for dx in range(2):
+                groups.setdefault((min(dz, 8 - dz), min(dy, 8 - dy), dx), []).append((dz, dy, dx))
+    order = sorted(groups, key=lambda k: -sum(k))
+    return [o for k in order for o in groups[k]][:-1]
+
+
 def exchange(
     tabs, pooled_in, pairs_in, slot_in, order_in, out, pairs, pooled, slot, order, lower, grads, send, landed, wide, total,
     own_sem, pooled_sem, slot_sem, order_sem, pair_send, pair_recv, row_send, row_recv, answers,
@@ -36,6 +46,7 @@
     parts = rows // PART
     me, col = lax.axis_index("tab"), lax.axis_index("col")
     plane = me // PLANE
+    z, y, x = me // 16, (me // 2) % 8, me % 2
     sibling = col + 1 - 2 * (col % 2)
     across = (col + 2) % 4
 
@@ -143,8 +154,8 @@
                 pl.semaphore_wait(answers, tabs - 1 - me)
 
 
-        def start(i, carry):
-            to = (me + i * STRIDE) % tabs
+        for dz, dy, dx in by_distance():
+            to = ((z + dz) % 8) * 16 + ((y + dy) % 8) * 2 + (x + dx) % 2
             pltpu.make_async_remote_copy(
                 src_ref=send.at[to, span],
                 dst_ref=landed.at[part, me],
@@ -153,9 +164,6 @@
                 device_id={"tab": to},
                 device_id_type=MESH,
             ).start()
-            return carry
-
-        lax.fori_loop(1, tabs, start, 0)
         pltpu.make_async_copy(send.at[me, span], landed.at[part, me], row_recv.at[part * planes + plane]).start()
 
     get_slot.wait()

time: 56 us -> 54.6 us (0.975)
  the two profiles are of different devices: /device:TPU:8 before, /device:TPU:1 now
where the time goes in v4:
time: 54.6 us; the launch traced here: 54.4 us
  Pallas kernels  52.2 us (96%)
  local copies, waits for them, and re-layouts  2.26 us (4%)
    pallas_call x1, Pallas kernels, per_device(): pl.pallas_call(functools.partial(exchange, tabs), out_shape=jax.ShapeDtyp...  52.2 us
    unnamed x1, local copies, waits for them, and re-layouts  2.26 us

profile of v4, /device:TPU:1, one launch (start us, length us, event | category | flops | bytes accessed | tf_op | source)
XLA Modules:
  0.0 54.4 jit_solution(15081188239449284679)
XLA Ops:
  0.0 52.2 %exchange.1 = bf16[4096,128]{1,0:T(8,128)(2,1)} custom-call(bf16[32,128,128]{2,1,0:T(8,128)(2,1)} %pooled_in.1, bf16[32,2032]{1,0:T(8,128)(2,1)} %pairs_in.1, s32[32,128]{1,0:T(8,128)} %bitcast.3, s32[128]{0:T(128)} %order_in.1), custom_call_target="tpu_custom_call" | custom-call | tf_op jit(solution)/shard_map/exchange/pallas_call | solution.py:223
  52.2 2.3 %copy.6 = bf16[1,4096,128]{2,1,0:T(8,128)(2,1)} copy(bf16[1,4096,128]{2,1,0:T(8,128)(2,1)} %bitcast.2) | data formatting | bytes 2097152

commit v5 on v4

--- a/solution.py
+++ b/solution.py
@@ -12,7 +12,6 @@
 PART = 16
 PLANE = 16
 BLOCK = 1024
-SECOND = 4096
 STRIDE = 77
 
 
@@ -38,7 +37,7 @@
 
 
 def exchange(
-    tabs, pooled_in, pairs_in, slot_in, order_in, out, pairs, pooled, slot, order, lower, grads, send, landed, wide, total,
+    tabs, pooled_in, pairs_in, slot_in, order_in, out, pairs, pooled, slot, order, lower, grads, send, landed, wide, side, total,
     own_sem, pooled_sem, slot_sem, order_sem, pair_send, pair_recv, row_send, row_recv, answers,
 ):
     rows, tables, _ = pooled.shape
@@ -136,17 +135,14 @@
         if part == 0:
             get_pooled.wait()
             get_order.wait()
-        lax.fori_loop(part * PART, (part + 1) * PART, multiply, 0, unroll=8)
+        lax.fori_loop(part * PART, (part + 1) * PART, multiply, 0, unroll=16)
 
         def place(k, carry):
             send[k, span] = grads[order[k]][part * PART : (part + 1) * PART].astype(jnp.bfloat16)
             return carry
 
-        lax.fori_loop(0, tables, place, 0, unroll=8)
-
-        if part + 1 < parts:
-            direct[part + 1].wait_recv()
-            passed.append(pass_pairs(2, part + 1, across, sibling))
+        lax.fori_loop(0, tables, place, 0, unroll=16)
+
         if part == 0:
 
             @pl.when(me < tabs - 1)
@@ -164,15 +160,20 @@
                 device_id={"tab": to},
                 device_id_type=MESH,
             ).start()
+        if part + 1 < parts:
+            direct[part + 1].wait_recv()
+            passed.append(pass_pairs(2, part + 1, across, sibling))
         pltpu.make_async_copy(send.at[me, span], landed.at[part, me], row_recv.at[part * planes + plane]).start()
 
     get_slot.wait()
     at = slot[...]
     key = (at // PART % parts) * (tabs * PART // 2) + at // (2 * PLANE * rows) * (PLANE * PART)
     key += at // rows % PLANE * PART + at % PART
-    slot[...] = key + at // (PLANE * rows) % 2 * SECOND
+    slot[...] = key
+    half = at // (PLANE * rows) % 2
     for i in range(slot.shape[0]):
         wide[pl.ds(i * LANES, LANES), :] = jnp.broadcast_to(slot[pl.ds(i, 1), :], (LANES, LANES)).T
+        side[pl.ds(i * LANES, LANES), :] = jnp.broadcast_to(half[i : i + 1, :], (LANES, LANES)).T
     total[...] = jnp.zeros_like(total)
 
     lane_id = lax.broadcasted_iota(jnp.int32, (1, LANES), 1)
@@ -191,13 +192,11 @@
         def add(b, c):
             at = pl.ds(pl.multiple_of(b * BLOCK, BLOCK), BLOCK)
             wanted = wide[at, :]
-            second = wanted >= SECOND
-            wanted = jnp.where(second, wanted - SECOND, wanted)
             picks = jnp.concatenate(
                 [jnp.where(wanted == ids, jnp.bfloat16(1), jnp.bfloat16(0)) for ids in row_ids], axis=1
             )
             both = jnp.dot(picks, held, preferred_element_type=jnp.float32)
-            total[at, :] += jnp.where(second, both[:, LANES:], both[:, :LANES])
+            total[at, :] += jnp.where(side[at, :] > 0, both[:, LANES:], both[:, :LANES])
             return c
 
         lax.fori_loop(0, tabs * rows // BLOCK, add, 0, unroll=4)
@@ -235,6 +234,7 @@
             pltpu.VMEM((tables, rows, width), jnp.bfloat16),
             pltpu.VMEM((parts, tabs, PART, width), jnp.bfloat16),
             pltpu.VMEM((total, LANES), jnp.int32),
+            pltpu.VMEM((total, LANES), jnp.int32),
             pltpu.VMEM((total, width), jnp.float32),
             pltpu.SemaphoreType.DMA,
             pltpu.SemaphoreType.DMA,

time: 54.6 us -> 54.2 us (level)
  no operation moved by 1% of the time
where the time goes in v5:
time: 54.2 us; the launch traced here: 54 us
  Pallas kernels  51.8 us (96%)
  local copies, waits for them, and re-layouts  2.26 us (4%)
    pallas_call x1, Pallas kernels, per_device(): pl.pallas_call(functools.partial(exchange, tabs), out_shape=jax.ShapeDtyp...  51.8 us
    unnamed x1, local copies, waits for them, and re-layouts  2.26 us

profile of v5, /device:TPU:1, one launch (start us, length us, event | category | flops | bytes accessed | tf_op | source)
XLA Modules:
  0.0 54.0 jit_solution(13864507892207916191)
XLA Ops:
  0.0 51.8 %exchange.1 = bf16[4096,128]{1,0:T(8,128)(2,1)} custom-call(bf16[32,128,128]{2,1,0:T(8,128)(2,1)} %pooled_in.1, bf16[32,2032]{1,0:T(8,128)(2,1)} %pairs_in.1, s32[32,128]{1,0:T(8,128)} %bitcast.3, s32[128]{0:T(128)} %order_in.1), custom_call_target="tpu_custom_call" | custom-call | tf_op jit(solution)/shard_map/exchange/pallas_call | solution.py:222
  51.8 2.3 %copy.6 = bf16[1,4096,128]{2,1,0:T(8,128)(2,1)} copy(bf16[1,4096,128]{2,1,0:T(8,128)(2,1)} %bitcast.2) | data formatting | bytes 2097152
